TPU v7x, 512 devices: a whole 4x4x16 slice. The times are simulated.
512 devices in a mesh: rows: 128 (over y, z, core), serve: 4 (over x).
Axes of the slice: x: 4, y: 4, z: 16, core: 2. Of those that a mesh axis runs over, the one named last changes fastest.
Arguments:
- table_rows: float32 [131072, 128], P('rows'), may hold values from -3 to 3
- row_accum: float32 [131072], P('rows'), may hold values from 0.002 to 0.05
- lookup_rows: int32 [4, 128, 1536], P('serve', 'rows'), may hold values from 0 to 1023
- bag_lengths: int32 [4, 128, 512], P('serve', 'rows'), may hold values from 1 to 8, 1536 in all within a row
- bag_owner: int32 [4, 128, 512, 1], P('serve', 'rows'), may hold values from 0 to 127; in each aligned block of 512 rows (0 to 511, 512 to 1023, ..., all dimensions but the last counted through in order) at most 8 rows name the same one
- bag_target: int32 [4, 128, 512], P('serve', 'rows'), may hold values from 0 to 3327
- bottom_in: bfloat16 [4, 16384, 256], P('serve', 'rows'), may hold values from -6 to 6
- labels: int32 [4, 16384], P('serve', 'rows'), may hold values 0 or 1
- w_bottom: bfloat16 [256, 128], replicated, may hold values from -0.375 to 0.375
- cross_u: bfloat16 [3456, 256], replicated, may hold values from -0.109375 to 0.109375
- cross_v: bfloat16 [256, 3456], replicated, may hold values from -0.375 to 0.375
- cross_bias: float32 [3456], replicated, may hold values from -3 to 3
- w_out: float32 [3456], replicated, may hold values from -0.109375 to 0.109375
- serve_owner: int32 [131072, 1], P('rows'), may hold values from 0 to 127; in each aligned block of 1024 rows (0 to 1023, 1024 to 2047, ...) at most 16 rows name the same one
Outputs:
- new_rows: float32 [131072, 128], P('rows', 'serve')
- new_accum: float32 [131072], P('rows')
- serving_delta: bfloat16 [128, 128, 16, 128], P('rows', None, None, 'serve')
- grad_bottom: float32 [256, 128], replicated
Inputs may be any that keep to these rules, and one draw needn't show every extreme that they name: `bag_lengths`: for each s and r the 512 lengths sum to 1536. `bag_owner`: among the 512 partial bags of one device no owner occurs more than 8 times, and on some device one owner occurs exactly 8 times. `serve_owner`: among the 1024 rows of one row shard no serving owner occurs more than 16 times, and on some shard one occurs exactly 16 times.
All inputs are finite; a program needn't handle non-finite values. No bound on the sum of `labels` on one device may be relied on, other than what follows from the above.
Results may differ from a plain program's by a relative error of at most 0.0057.
Values may be sent and summed in bfloat16 or wider, within the bound.
No kernel may reach another device: no remote copies, remote signals or barrier semaphores. Data moves between devices by JAX's collectives and lax.ppermute only.
A program may use at most 64 MiB of HBM per device.

v0:
```python
import functools

import jax
import jax.numpy as jnp
from jax import lax
from jax.experimental import pallas as pl
from jax.experimental.pallas import tpu as pltpu
from jax.sharding import PartitionSpec as P

TABLES = 26
LEARN_RATE = 0.1
EMB = 128
PEERS = 128
CAP = 8
ROWS_A = 10
ALL_A = PEERS * ROWS_A
ROWS_D = 6
ALL_D = PEERS * ROWS_D
F32 = jnp.float32
BF16 = jnp.bfloat16
VMEM_LIMIT = 32 * 1024 * 1024


def dot(a, b, ca=1, cb=0):
    return lax.dot_general(a, b, (((ca,), (cb,)), ((), ())), preferred_element_type=F32)


def iota(shape, dim):
    return lax.broadcasted_iota(jnp.int32, shape, dim)


def onehot(mask):
    return jnp.where(mask, 1.0, 0.0).astype(BF16)


def divide_floor(values, by):
    return jnp.floor((values.astype(F32) + 0.5) * (1.0 / by)).astype(jnp.int32)


def owner_place(owners):
    return owners


def fetch(sources, targets, sems):
    copies = [pltpu.make_async_copy(s, t, sems.at[i]) for i, (s, t) in enumerate(zip(sources, targets))]
    for copy in copies:
        copy.start()
    return copies


def bag_ends(lengths_ref):
    bags = lengths_ref.shape[1]
    row_id = iota((bags, bags), 0)
    col_id = iota((bags, bags), 1)
    lens = jnp.broadcast_to(lengths_ref[...].astype(F32), (8, bags)).astype(BF16)
    starts = dot(onehot(col_id < row_id), lens, 1, 1)[:, 0:1].astype(jnp.int32)
    ends = dot(onehot(col_id <= row_id), lens, 1, 1)[:, 0:1].astype(jnp.int32)
    return starts, ends


def pool_kernel(
    lengths_hbm,
    lookups_hbm,
    owners_hbm,
    targets_hbm,
    table_hbm,
    out_ref,
    slots_ref,
    lengths_ref,
    lookups_ref,
    owners_ref,
    targets_ref,
    table_ref,
    sems,
):
    copies = fetch(
        (lengths_hbm, lookups_hbm, owners_hbm, targets_hbm, table_hbm),
        (lengths_ref, lookups_ref, owners_ref, targets_ref, table_ref),
        sems,
    )
    bags = lengths_ref.shape[1]
    looks = lookups_ref.shape[1]
    touched = table_ref.shape[0]
    for copy in copies[:4]:
        copy.wait()
    owners = owners_ref[...]
    of_owner = jnp.where(iota((PEERS, bags), 0) == owners, 1.0, 0.0)
    before = dot(of_owner.astype(BF16), onehot(iota((bags, bags), 0) < iota((bags, bags), 1)))
    rank = jnp.sum(before * of_owner, axis=0, keepdims=True).astype(jnp.int32)
    slots = owner_place(owners) * ROWS_A + rank
    slots_ref[...] = slots
    targets = targets_ref[...]
    sample = divide_floor(targets, TABLES)
    table_of = targets - sample * TABLES
    lane = iota((EMB, bags), 0)
    names = jnp.where(lane == rank, sample + 1, 0) + jnp.where(lane == rank + CAP, table_of, 0)
    names = dot(of_owner.astype(BF16), names.astype(F32).astype(BF16), 1, 1).astype(BF16)
    copies[4].wait()
    table = table_ref[...]
    high = table.astype(BF16)
    low = (table - high.astype(F32)).astype(BF16)
    starts, ends = bag_ends(lengths_ref)
    place = iota((bags, looks), 1)
    in_bag = onehot((place >= starts) & (place < ends))
    lookups = jnp.broadcast_to(lookups_ref[...].astype(F32), (128, looks)).T.astype(jnp.int32)
    both = jnp.concatenate([high, low], axis=1)
    lane = iota((512, 128), 1)
    sums = 0.0
    for first in range(0, looks, 512):
        part = lookups[first : first + 512]
        goes = jnp.concatenate([onehot(part == lane + c) for c in range(0, touched, 128)], axis=1)
        sums = sums + dot(in_bag[:, first : first + 512], dot(goes, both).astype(BF16))
    pooled = (sums[:, :EMB] + sums[:, EMB:]).astype(BF16)
    payload = dot(onehot(iota((ALL_A, bags), 0) == slots), pooled)
    ninth = onehot(iota((ALL_A, PEERS), 0) == owner_place(iota((ALL_A, PEERS), 1)) * ROWS_A + CAP)
    out_ref[...] = (payload + dot(ninth, names)).astype(BF16)


def ready_kernel(
    lengths_ref,
    lookups_ref,
    slots_ref,
    owners_ref,
    table_ref,
    cross_u_ref,
    routed_ref,
    steps_ref,
    block_ref,
    cols_ref,
    u_turned_ref,
    turned_ref,
):
    rows = owners_ref.shape[1]
    bags = slots_ref.shape[1]
    looks = lookups_ref.shape[1]
    u_turned_ref[...] = cross_u_ref[...].T
    starts, ends = bag_ends(lengths_ref)
    place = iota((bags, looks), 1)
    in_bag = onehot((place >= starts) & (place < ends))
    of_row = onehot(iota((rows, looks), 0) == lookups_ref[...])
    counts = dot(in_bag, of_row, 1, 1).astype(BF16)
    routed_ref[...] = dot(onehot(iota((ALL_A, bags), 0) == slots_ref[...]), counts).astype(BF16)
    owners = owners_ref[...]
    of_owner = jnp.where(iota((PEERS, rows), 0) == owners, 1.0, 0.0)
    before = dot(of_owner.astype(BF16), onehot(iota((rows, rows), 0) < iota((rows, rows), 1)))
    rank = jnp.sum(before * of_owner, axis=0, keepdims=True).astype(jnp.int32)
    row_of = lax.shift_right_logical(rank, 2)
    block_ref[...] = rank - 4 * row_of
    steps_ref[...] = onehot(iota((ALL_D, rows), 0) == owner_place(owners) * ROWS_D + row_of)
    turned_ref[...] = table_ref[...].T
    cols = cols_ref.shape[0]
    cols_ref[...] = turned_ref[pl.ds(pl.multiple_of(lax.axis_index("serve") * cols, cols), cols), :]


def owner_kernel(*refs):
    arrived_ref, *refs = refs
    count = (len(refs) - 8) // 2
    sources, out_ref = refs[:count], refs[count]
    targets = refs[count + 1 : 2 * count + 1]
    cross_ref, mixed_ref, embed_ref, member_ref, table_ref, wanted_ref, sems = refs[2 * count + 1 :]
    copies = [pltpu.make_async_copy(s, t, sems.at[i]) for i, (s, t) in enumerate(zip(sources, targets))]
    dense_ref, w_bottom_ref, cross_u_ref, bias_ref, w_out_ref, labels_ref, cross_v_ref, u_turned_ref = targets
    for copy in copies[:7]:
        copy.start()
    samples = dense_ref.shape[0]
    peer = iota((PEERS, ALL_A), 0) * ROWS_A
    slot = iota((PEERS, ALL_A), 1)
    name_row = onehot(slot == peer + CAP)
    chunk = onehot((slot >= peer) & (slot < peer + ROWS_A))
    arrived = arrived_ref[...]
    names = dot(name_row, arrived).astype(BF16)
    spread = dot(names, chunk, 0, 0)
    place = iota((CAP, ALL_A), 1)
    place = place - divide_floor(place, ROWS_A) * ROWS_A
    picks = iota((CAP, ALL_A), 0) == place
    sample_row = jnp.sum(jnp.where(picks, spread[:CAP], 0.0), axis=0, keepdims=True)
    table_row = jnp.sum(jnp.where(picks, spread[CAP : 2 * CAP], 0.0), axis=0, keepdims=True)
    member_f = jnp.where(sample_row.astype(jnp.int32) == iota((samples, ALL_A), 0) + 1, 1.0, 0.0)
    member = member_f.astype(BF16)
    member_ref[...] = member_f.T.astype(BF16)
    table_ref[...] = jnp.broadcast_to(table_row, (samples, ALL_A)).T.astype(BF16)

    for copy in copies[:2]:
        copy.wait()
    dense = dense_ref[...]
    pre_act = dot(dense, w_bottom_ref[...])
    sigma = jax.nn.sigmoid(pre_act)
    cross_ref[:, :EMB] = (pre_act * sigma).astype(BF16)
    table_t = table_ref[...]
    for t in range(0, TABLES, 2):
        if t == 16:
            copies[7].start()
        both = [jnp.where(table_t == t + u, arrived, 0.0).astype(BF16) for u in range(2)]
        cross_ref[:, (t + 1) * EMB : (t + 3) * EMB] = dot(member, jnp.concatenate(both, axis=1)).astype(BF16)

    for copy in copies[2:7]:
        copy.wait()
    low_rank = dot(cross_ref[...], cross_u_ref[...]).astype(BF16)
    w_out = w_out_ref[...]
    mixed_ref[...] = (dot(low_rank, cross_v_ref[...]) + (bias_ref[...] + 1.0)) * w_out
    cross_f = cross_ref[...].astype(F32)
    logits = jnp.sum(cross_f * mixed_ref[...], axis=1, keepdims=True)
    logit_grad = jax.nn.sigmoid(logits) - labels_ref[...].astype(F32)
    mix_grad = (logit_grad * w_out * cross_f).astype(BF16)
    low_grad = dot(mix_grad, cross_v_ref[...], 1, 1).astype(BF16)
    copies[7].wait()
    in_grad = logit_grad * mixed_ref[...] + dot(low_grad, u_turned_ref[...])
    pre_grad = (in_grad[:, :EMB] * (sigma * (1.0 + pre_act * (1.0 - sigma)))).astype(BF16)
    for t in range(TABLES):
        embed_ref[t * samples : (t + 1) * samples, :] = in_grad[:, (t + 1) * EMB : (t + 2) * EMB].astype(BF16)
    line = iota((1, 2 * PEERS), 1)
    line = lax.shift_right_logical(line, 1) * ROWS_A + CAP + (line & 1)
    wanted_ref[...] = onehot(iota((ALL_A, 2 * PEERS), 0) == line)
    embed_ref[TABLES * samples :, :] = dot(dense, pre_grad, 0, 0).astype(BF16)

    step = ALL_A // 2
    for c in range(ALL_A // step):
        rows = slice(c * step, (c + 1) * step)
        member_c = member_ref[rows, :]
        table_c = table_ref[rows, :]
        wide = [jnp.where(table_c == t, member_c, 0.0).astype(BF16) for t in range(TABLES)]
        wide = jnp.concatenate(wide + [wanted_ref[rows, :]], axis=1)
        out_ref[rows, :] = dot(wide, embed_ref[...]).astype(BF16)


def return_kernel(returned_ref, routed_ref, grads_ref, bottom_ref):
    returned = returned_ref[...]
    grads_ref[...] = dot(returned, routed_ref[...], 0, 0).astype(BF16)
    slot = iota((8, ALL_A), 1)
    place = slot - divide_floor(slot, ROWS_A) * ROWS_A
    bottom_ref[...] = dot(onehot(place == iota((8, ALL_A), 0) + CAP), returned)


def total_kernel(grads_ref, bottom_ref, total_ref, message_ref):
    total = grads_ref[0].astype(F32)
    for s in range(1, grads_ref.shape[0]):
        total = total + grads_ref[s].astype(F32)
    total_ref[...] = total
    squares = jnp.sum(total * total, axis=0, keepdims=True)
    bottom = bottom_ref[...]
    message = jnp.concatenate([squares, bottom[0:1], bottom[1:2]], axis=1)
    for s in range(message_ref.shape[0]):
        message_ref[s] = message


def step_kernel(
    message_ref, total_ref, accum_ref, table_ref, steps_ref, block_ref, rows_ref, accum_out_ref, out_ref
):
    rows = accum_ref.shape[1]
    message = message_ref[0]
    for s in range(1, message_ref.shape[0]):
        message = message + message_ref[s]
    accum = accum_ref[...] + message[:, :rows] * (1.0 / EMB)
    accum_out_ref[...] = accum
    step = total_ref[...] * (1.0 / jnp.sqrt(accum))
    rows_ref[...] = table_ref[...] - LEARN_RATE * step
    block = block_ref[...]
    wide = jnp.concatenate([jnp.where(block == a, step, 0.0) for a in range(4)], axis=0).astype(BF16)
    payload = dot(steps_ref[...], wide, 1, 1)
    slot = iota((ALL_D, EMB), 0)
    place = slot - divide_floor(slot, ROWS_D) * ROWS_D
    payload = jnp.where(place == 4, message[:, rows : rows + EMB], payload)
    payload = jnp.where(place == 5, message[:, rows + EMB : rows + 2 * EMB], payload)
    out_ref[...] = payload.astype(BF16)


def final_kernel(served_ref, serving_ref, bottom_ref):
    served = served_ref[...]
    slot = iota((ALL_D, PEERS), 0)
    peer = iota((ALL_D, PEERS), 1)
    for r in range(4):
        pick = onehot(slot == peer * ROWS_D + r)
        serving_ref[r * EMB : (r + 1) * EMB, :] = dot(served, pick, 0, 0).astype(BF16)
    line = iota((2 * PEERS, ALL_D), 0)
    slot = iota((2 * PEERS, ALL_D), 1)
    pick = onehot(slot == lax.shift_right_logical(line, 1) * ROWS_D + 4 + (line & 1))
    bottom_ref[...] = dot(pick, served)


def call(kernel, outs, *args, scratch=(), flops=0, hbm=(), limit=VMEM_LIMIT):
    moved = sum(x.size * x.dtype.itemsize for x in args)
    spaces = [pltpu.HBM if i in hbm else pltpu.VMEM for i in range(len(args))]
    return pl.pallas_call(
        kernel,
        out_shape=[jax.ShapeDtypeStruct(shape, kind) for shape, kind in outs],
        in_specs=[pl.BlockSpec(memory_space=space) for space in spaces],
        scratch_shapes=list(scratch),
        compiler_params=pltpu.CompilerParams(vmem_limit_bytes=limit),
        cost_estimate=pl.CostEstimate(flops=flops, bytes_accessed=moved, transcendentals=0),
    )(*args)


def over_rows(chunks, rows):
    split = chunks.reshape(PEERS, rows // 2, 2, EMB)
    split = lax.all_to_all(split, "rows", split_axis=0, concat_axis=0, tiled=True)
    return split.reshape(PEERS * rows, EMB)


def over_serve(pieces):
    return lax.all_to_all(pieces, "serve", split_axis=0, concat_axis=0, tiled=True)


def per_device(
    table_rows,
    row_accum,
    lookup_rows,
    bag_lengths,
    bag_owner,
    bag_target,
    bottom_in,
    labels,
    w_bottom,
    cross_u,
    cross_v,
    cross_bias,
    w_out,
    serve_owner,
):
    touched = table_rows.shape[0]
    lookups = lookup_rows.reshape(1, -1)
    lengths = bag_lengths.reshape(1, -1)
    bags = lengths.shape[1]
    owners = bag_owner.reshape(1, -1)
    targets = bag_target.reshape(1, -1)
    dense_in = bottom_in.reshape(-1, bottom_in.shape[-1])
    samples = dense_in.shape[0]
    width = cross_u.shape[0]
    serves = lax.axis_size("serve")
    cols = EMB // serves

    outgoing, slots = call(
        pool_kernel,
        [((ALL_A, EMB), BF16), ((1, bags), jnp.int32)],
        lengths,
        lookups,
        owners,
        targets,
        table_rows,
        scratch=(
            pltpu.VMEM(lengths.shape, jnp.int32),
            pltpu.VMEM(lookups.shape, jnp.int32),
            pltpu.VMEM(owners.shape, jnp.int32),
            pltpu.VMEM(targets.shape, jnp.int32),
            pltpu.VMEM(table_rows.shape, F32),
            pltpu.SemaphoreType.DMA((5,)),
        ),
        flops=2 * 700 * 10**6,
        hbm=range(5),
        limit=60 * 1024 * 1024,
    )
    arrived = over_rows(outgoing, ROWS_A)
    routed, steps_to, block, table_cols, u_turned = call(
        ready_kernel,
        [
            ((ALL_A, touched), BF16),
            ((ALL_D, touched), BF16),
            ((1, touched), jnp.int32),
            ((cols, touched), F32),
            (cross_u.shape[::-1], BF16),
        ],
        lengths,
        lookups,
        slots,
        serve_owner.reshape(1, -1),
        table_rows,
        cross_u,
        scratch=(pltpu.VMEM((EMB, touched), F32),),
        flops=2 * 1600 * 10**6,
        limit=60 * 1024 * 1024,
    )
    operands = (
        arrived,
        dense_in,
        w_bottom,
        cross_u,
        cross_bias.reshape(1, -1),
        w_out.reshape(1, -1),
        labels.reshape(-1, 1),
        cross_v,
        u_turned,
    )
    (replies,) = call(
        owner_kernel,
        [((ALL_A, EMB), BF16)],
        *operands,
        scratch=tuple(pltpu.VMEM(x.shape, x.dtype) for x in operands[1:])
        + (
            pltpu.VMEM((samples, width), BF16),
            pltpu.VMEM((samples, width), F32),
            pltpu.VMEM((samples * TABLES + 2 * PEERS, EMB), BF16),
            pltpu.VMEM((ALL_A, PEERS), BF16),
            pltpu.VMEM((ALL_A, PEERS), BF16),
            pltpu.VMEM((ALL_A, 2 * PEERS), BF16),
            pltpu.SemaphoreType.DMA((len(operands) - 1,)),
        ),
        flops=2 * 1600 * 10**6,
        hbm=range(1, len(operands)),
        limit=52 * 1024 * 1024,
    )
    returned = over_rows(replies, ROWS_A)
    grads, bottom = call(
        return_kernel,
        [((EMB, touched), BF16), ((8, EMB), F32)],
        returned,
        routed,
        flops=2 * 160 * 10**6,
    )
    pieces = over_serve(grads.reshape(serves, cols, touched))
    total, message = call(
        total_kernel,
        [((cols, touched), F32), ((serves, 1, touched + 2 * EMB), F32)],
        pieces,
        bottom,
    )
    messages = over_serve(message)
    new_rows, new_accum, steps = call(
        step_kernel,
        [((cols, touched), F32), ((1, touched), F32), ((ALL_D, EMB), BF16)],
        messages,
        total,
        row_accum.reshape(1, -1),
        table_cols,
        steps_to,
        block,
        flops=2 * 100 * 10**6,
    )
    served = over_rows(steps, ROWS_D)
    serving, grad_bottom = call(
        final_kernel, [((4 * EMB, PEERS), BF16), ((2 * PEERS, EMB), F32)], served, flops=2 * 50 * 10**6
    )
    serving = serving.reshape(16, cols, PEERS).transpose(2, 0, 1)[None]
    return (new_rows.T, new_accum.reshape(-1), serving, grad_bottom)


def solution(mesh):
    return jax.shard_map(
        per_device,
        mesh=mesh,
        in_specs=(
            P("rows", None),
            P("rows"),
            P("serve", "rows", None),
            P("serve", "rows", None),
            P("serve", "rows", None, None),
            P("serve", "rows", None),
            P("serve", "rows", None),
            P("serve", "rows"),
            P(),
            P(),
            P(),
            P(),
            P(),
            P("rows", None),
        ),
        out_specs=(P("rows", "serve"), P("rows"), P("rows", None, None, "serve"), P()),
        check_vma=False,
    )
```

profile of v0, /device:TPU:1, one launch (start us, length us, event | category | flops | bytes accessed | tf_op | source)
XLA Modules:
  0.0 139.3 jit_solution(11527436199069528208)
XLA Ops:
  0.6 0.0 copy-start.7
  0.6 0.0 copy-start.8
  0.7 0.0 copy-start.9
  0.7 4.3 %shard_map.165 = (bf16[1280,128]{1,0:T(8,128)(2,1)}, s32[1,512]{1,0:T(1,128)}) custom-call(s32[1,512]{1,0:T(1,128)} %bitcast.39, s32[1,1536]{1,0:T(1,128)} %bitcast.33, s32[1,512]{1,0:T(1,128)} %bitcast.37, s32[1,512]{1,0:T(1,128)} %bitcast.38, f32[1024,128]{1,0:T(8,128)} %table_ref.1), custom_call_target="tpu_custom_call" | custom-call | flops 1400000000 | bytes 536576 | tf_op jit(solution)/shard_map/pallas_call | solution.py:283
  5.0 20.6 %all-to-all-start = ((bf16[128,5,2,128]{3,2,1,0:T(2,128)(2,1)}), bf16[128,5,2,128]{3,2,1,0:T(2,128)(2,1)S(1)}, u32[]{:S(2)}, u32[]{:S(2)}) async-start(bf16[128,5,2,128]{3,2,1,0:T(2,128)(2,1)} %bitcast.30), calls=%async_computation | async-start | bytes 655360 | tf_op jit(solution)/shard_map/all_to_all | solution.py:295
  25.6 0.0 copy-done.7
  25.6 0.0 copy-done.8
  25.6 0.0 copy-done.9
  25.7 0.1 copy.18.refs_6_
  25.8 0.0 copy-start.6
  25.8 8.3 %shard_map.166 = (bf16[1280,1024]{1,0:T(8,128)(2,1)}, bf16[768,1024]{1,0:T(8,128)(2,1)}, s32[1,1024]{1,0:T(1,128)}, f32[32,1024]{1,0:T(8,128)}, bf16[256,3456]{1,0:T(8,128)(2,1)}) custom-call(s32[1,512]{1,0:T(1,128)} %bitcast.40, s32[1,1536]{1,0:T(1,128)} %bitcast.34, s32[1,512]{1,0:T(1,128)} %get-tuple-element.21.slots_ref, s32[1,1024]{1,0:T(1,128)} %bitcast.35, ...), custom_call_target="tpu_custom_call" | custom-call | flops 3200000000 | bytes 2308096 | tf_op jit(solution)/shard_map/pallas_call | solution.py:283
  34.1 16.9 %all-to-all-done = bf16[128,5,2,128]{3,2,1,0:T(2,128)(2,1)S(1)} async-done(((bf16[128,5,2,128]{3,2,1,0:T(2,128)(2,1)}), bf16[128,5,2,128]{3,2,1,0:T(2,128)(2,1)S(1)}, u32[]{:S(2)}, u32[]{:S(2)}) %all-to-all-start) | async-done | bytes 327712 | tf_op jit(solution)/shard_map/all_to_all | solution.py:295
  51.0 8.8 %shard_map.167 = bf16[1280,128]{1,0:T(8,128)(2,1)S(1)} custom-call(bf16[1280,128]{1,0:T(8,128)(2,1)S(1)} %bitcast.23, bf16[128,256]{1,0:T(8,128)(2,1)S(1)} %bitcast.29, bf16[256,128]{1,0:T(8,128)(2,1)S(1)} %copy-done.6, bf16[3456,256]{1,0:T(8,128)(2,1)} %refs_3_.1, f32[1,3456]{1,0:T(1,128)S(1)} %reshape.72.refs_4_, f32[1,3456]{1,0:T(1,128)S(1)} %reshape.73.refs_5_, ...), custom_call_target="tpu_custom_call" | custom-call | flops 3200000000 | bytes 5795328 | tf_op jit(solution)/shard_map/pallas_call | solution.py:283
  59.8 32.1 %all_to_all.25 = bf16[128,5,2,128]{3,2,1,0:T(2,128)(2,1)S(1)} all-to-all(bf16[128,5,2,128]{3,2,1,0:T(2,128)(2,1)S(1)} %bitcast.24), channel_id=1, replica_groups=mesh['rows'=128,'serve'=4] {'rows'}, dimensions={0} | all-to-all | bytes 655360 | tf_op jit(solution)/shard_map/all_to_all | solution.py:295
  91.9 0.0 copy-done
  91.9 0.0 copy-start.4
  91.9 0.6 shard_map.168
  92.5 9.3 %all_to_all.26.grads_ref = bf16[4,32,1024]{2,1,0:T(8,128)(2,1)S(1)} all-to-all(bf16[4,32,1024]{2,1,0:T(8,128)(2,1)S(1)} %bitcast.25), channel_id=1, replica_groups=mesh['rows'=128,'serve'=4] {'serve'}, dimensions={0} | all-to-all | bytes 524288 | tf_op jit(solution)/shard_map/all_to_all | solution.py:300
  101.9 0.1 shard_map.169
  101.9 6.6 %all_to_all.27.message_ref = f32[4,1,1280]{2,1,0:T(1,128)S(1)} all-to-all(f32[4,1,1280]{2,1,0:T(1,128)S(1)} %get-tuple-element.26), channel_id=1, replica_groups=mesh['rows'=128,'serve'=4] {'serve'}, dimensions={0} | all-to-all | bytes 40960 | tf_op jit(solution)/shard_map/all_to_all | solution.py:300
  108.5 0.0 copy-done.4
  108.5 0.7 shard_map.170
  109.2 28.9 %all_to_all.28 = bf16[128,3,2,128]{3,2,1,0:T(2,128)(2,1)S(1)} all-to-all(bf16[128,3,2,128]{3,2,1,0:T(2,128)(2,1)S(1)} %bitcast.26), channel_id=1, replica_groups=mesh['rows'=128,'serve'=4] {'rows'}, dimensions={0} | all-to-all | bytes 393216 | tf_op jit(solution)/shard_map/all_to_all | solution.py:295
  138.1 1.2 shard_map.171
  (12 shorter events, 0.0 us)
Async XLA Ops:
  0.6 25.0 %copy-start.7 = (f32[3456]{0:T(1024)S(1)}, f32[3456]{0:T(1024)}, u32[]{:S(2)}) copy-start(f32[3456]{0:T(1024)} %param.25) | copy-start | bytes 41476
  0.6 25.0 %copy-start.8 = (f32[3456]{0:T(1024)S(1)}, f32[3456]{0:T(1024)}, u32[]{:S(2)}) copy-start(f32[3456]{0:T(1024)} %param.26) | copy-start | bytes 41476
  0.7 25.0 %copy-start.9 = (s32[1,128]{1,0:T(1,128)S(1)}, s32[1,128]{1,0:T(1,128)}, u32[]{:S(2)}) copy-start(s32[1,128]{1,0:T(1,128)} %param.21) | copy-start | bytes 1540
  5.0 46.0 %all-to-all-start = ((bf16[128,5,2,128]{3,2,1,0:T(2,128)(2,1)}), bf16[128,5,2,128]{3,2,1,0:T(2,128)(2,1)S(1)}, u32[]{:S(2)}, u32[]{:S(2)}) async-start(bf16[128,5,2,128]{3,2,1,0:T(2,128)(2,1)} %bitcast.30), calls=%async_computation | async-start | bytes 655360 | tf_op jit(solution)/shard_map/all_to_all | solution.py:295
  25.8 25.2 %copy-start.5 = (bf16[1,128,256]{2,1,0:T(8,128)(2,1)S(1)}, bf16[1,128,256]{2,1,0:T(8,128)(2,1)}, u32[]{:S(2)}) copy-start(bf16[1,128,256]{2,1,0:T(8,128)(2,1)} %param.20) | copy-start | bytes 196612
  25.8 25.2 %copy-start.6 = (bf16[256,128]{1,0:T(8,128)(2,1)S(1)}, bf16[256,128]{1,0:T(8,128)(2,1)}, u32[]{:S(2)}) copy-start(bf16[256,128]{1,0:T(8,128)(2,1)} %refs_2_.1) | copy-start | bytes 196612
  51.0 40.9 %copy-start = (bf16[1280,1024]{1,0:T(8,128)(2,1)S(1)}, bf16[1280,1024]{1,0:T(8,128)(2,1)}, u32[]{:S(2)}) copy-start(bf16[1280,1024]{1,0:T(8,128)(2,1)} %get-tuple-element.23.routed_ref) | copy-start | bytes 7864324
  91.9 16.6 %copy-start.1 = (bf16[768,1024]{1,0:T(8,128)(2,1)S(1)}, bf16[768,1024]{1,0:T(8,128)(2,1)}, u32[]{:S(2)}) copy-start(bf16[768,1024]{1,0:T(8,128)(2,1)} %get-tuple-element.29.steps_ref) | copy-start | bytes 4718596
  91.9 16.6 %copy-start.2 = (f32[32,1024]{1,0:T(8,128)S(1)}, f32[32,1024]{1,0:T(8,128)}, u32[]{:S(2)}) copy-start(f32[32,1024]{1,0:T(8,128)} %get-tuple-element.28.table_ref) | copy-start | bytes 393220
  91.9 16.6 %copy-start.3 = (f32[1024]{0:T(1024)S(1)}, f32[1024]{0:T(1024)}, u32[]{:S(2)}) copy-start(f32[1024]{0:T(1024)} %param.15) | copy-start | bytes 12292
  91.9 16.6 %copy-start.4 = (s32[1,1024]{1,0:T(1,128)S(1)}, s32[1,1024]{1,0:T(1,128)}, u32[]{:S(2)}) copy-start(s32[1,1024]{1,0:T(1,128)} %get-tuple-element.30.block_ref) | copy-start | bytes 12292
where the time goes:
time: 140 us; the launch traced here: 139 us
  blocking collectives  76.9 us (55%)
  Pallas kernels  24 us (17%)
  starting transfers between devices  20.6 us (15%)
  waiting for transfers between devices  16.9 us (12%)
    all_to_all x2, blocking collectives, over_rows(): lax.all_to_all(split, 'rows', split_axis=0, concat_axis=0, tiled=True)  61 us
    pallas_call x7, Pallas kernels, call(): pl.pallas_call(kernel, out_shape=[jax.ShapeDtypeStruct(shape, kind) for s...  24 us
    all_to_all x1, starting transfers between devices, over_rows(): lax.all_to_all(split, 'rows', split_axis=0, concat_axis=0, tiled=True)  20.6 us
    all_to_all x1, waiting for transfers between devices, over_rows(): lax.all_to_all(split, 'rows', split_axis=0, concat_axis=0, tiled=True)  16.9 us
    all_to_all x2, blocking collectives, over_serve(): lax.all_to_all(pieces, 'serve', split_axis=0, concat_axis=0, tiled=True)  15.9 us
  transfers between devices with their start and end apart: 1, of which 1 were waited for; matrix products, arithmetic and copies ran while one was open for 0% of the time, Pallas kernels for 6%

commit v1 on v0

--- a/solution.py
+++ b/solution.py
@@ -17,6 +17,7 @@
 ROWS_D = 6
 ALL_D = PEERS * ROWS_D
 F32 = jnp.float32
+SMALL = jnp.int8
 BF16 = jnp.bfloat16
 VMEM_LIMIT = 32 * 1024 * 1024
 
@@ -122,24 +123,21 @@
     slots_ref,
     owners_ref,
     table_ref,
-    cross_u_ref,
     routed_ref,
     steps_ref,
     block_ref,
     cols_ref,
-    u_turned_ref,
     turned_ref,
 ):
     rows = owners_ref.shape[1]
     bags = slots_ref.shape[1]
     looks = lookups_ref.shape[1]
-    u_turned_ref[...] = cross_u_ref[...].T
     starts, ends = bag_ends(lengths_ref)
     place = iota((bags, looks), 1)
     in_bag = onehot((place >= starts) & (place < ends))
     of_row = onehot(iota((rows, looks), 0) == lookups_ref[...])
     counts = dot(in_bag, of_row, 1, 1).astype(BF16)
-    routed_ref[...] = dot(onehot(iota((ALL_A, bags), 0) == slots_ref[...]), counts).astype(BF16)
+    routed_ref[...] = dot(onehot(iota((ALL_A, bags), 0) == slots_ref[...]), counts).astype(jnp.int32).astype(SMALL)
     owners = owners_ref[...]
     of_owner = jnp.where(iota((PEERS, rows), 0) == owners, 1.0, 0.0)
     before = dot(of_owner.astype(BF16), onehot(iota((rows, rows), 0) < iota((rows, rows), 1)))
@@ -153,14 +151,15 @@
 
 
 def owner_kernel(*refs):
-    arrived_ref, *refs = refs
-    count = (len(refs) - 8) // 2
+    arrived_ref, _, *refs = refs
+    count = (len(refs) - 10) // 2
     sources, out_ref = refs[:count], refs[count]
     targets = refs[count + 1 : 2 * count + 1]
-    cross_ref, mixed_ref, embed_ref, member_ref, table_ref, wanted_ref, sems = refs[2 * count + 1 :]
+    cross_ref, mixed_ref, embed_ref, member_ref, table_ref, wanted_ref, *refs = refs[2 * count + 1 :]
+    u_turned_ref, v_turned_ref, sems = refs
     copies = [pltpu.make_async_copy(s, t, sems.at[i]) for i, (s, t) in enumerate(zip(sources, targets))]
-    dense_ref, w_bottom_ref, cross_u_ref, bias_ref, w_out_ref, labels_ref, cross_v_ref, u_turned_ref = targets
-    for copy in copies[:7]:
+    dense_ref, w_bottom_ref, cross_u_ref, bias_ref, w_out_ref, labels_ref, cross_v_ref = targets
+    for copy in copies:
         copy.start()
     samples = dense_ref.shape[0]
     peer = iota((PEERS, ALL_A), 0) * ROWS_A
@@ -188,13 +187,15 @@
     cross_ref[:, :EMB] = (pre_act * sigma).astype(BF16)
     table_t = table_ref[...]
     for t in range(0, TABLES, 2):
-        if t == 16:
-            copies[7].start()
+        if t == 14:
+            for copy in copies[2:6]:
+                copy.wait()
+            u_turned_ref[...] = cross_u_ref[...].T
         both = [jnp.where(table_t == t + u, arrived, 0.0).astype(BF16) for u in range(2)]
         cross_ref[:, (t + 1) * EMB : (t + 3) * EMB] = dot(member, jnp.concatenate(both, axis=1)).astype(BF16)
 
-    for copy in copies[2:7]:
-        copy.wait()
+    copies[6].wait()
+    v_turned_ref[...] = cross_v_ref[...].T
     low_rank = dot(cross_ref[...], cross_u_ref[...]).astype(BF16)
     w_out = w_out_ref[...]
     mixed_ref[...] = (dot(low_rank, cross_v_ref[...]) + (bias_ref[...] + 1.0)) * w_out
@@ -202,8 +203,7 @@
     logits = jnp.sum(cross_f * mixed_ref[...], axis=1, keepdims=True)
     logit_grad = jax.nn.sigmoid(logits) - labels_ref[...].astype(F32)
     mix_grad = (logit_grad * w_out * cross_f).astype(BF16)
-    low_grad = dot(mix_grad, cross_v_ref[...], 1, 1).astype(BF16)
-    copies[7].wait()
+    low_grad = dot(mix_grad, v_turned_ref[...]).astype(BF16)
     in_grad = logit_grad * mixed_ref[...] + dot(low_grad, u_turned_ref[...])
     pre_grad = (in_grad[:, :EMB] * (sigma * (1.0 + pre_act * (1.0 - sigma)))).astype(BF16)
     for t in range(TABLES):
@@ -225,7 +225,7 @@
 
 def return_kernel(returned_ref, routed_ref, grads_ref, bottom_ref):
     returned = returned_ref[...]
-    grads_ref[...] = dot(returned, routed_ref[...], 0, 0).astype(BF16)
+    grads_ref[...] = dot(returned, routed_ref[...].astype(BF16), 0, 0).astype(BF16)
     slot = iota((8, ALL_A), 1)
     place = slot - divide_floor(slot, ROWS_A) * ROWS_A
     bottom_ref[...] = dot(onehot(place == iota((8, ALL_A), 0) + CAP), returned)
@@ -349,27 +349,26 @@
         limit=60 * 1024 * 1024,
     )
     arrived = over_rows(outgoing, ROWS_A)
-    routed, steps_to, block, table_cols, u_turned = call(
+    routed, steps_to, block, table_cols = call(
         ready_kernel,
         [
-            ((ALL_A, touched), BF16),
+            ((ALL_A, touched), SMALL),
             ((ALL_D, touched), BF16),
             ((1, touched), jnp.int32),
             ((cols, touched), F32),
-            (cross_u.shape[::-1], BF16),
         ],
         lengths,
         lookups,
         slots,
         serve_owner.reshape(1, -1),
         table_rows,
-        cross_u,
         scratch=(pltpu.VMEM((EMB, touched), F32),),
         flops=2 * 1600 * 10**6,
         limit=60 * 1024 * 1024,
     )
     operands = (
         arrived,
+        steps_to,
         dense_in,
         w_bottom,
         cross_u,
@@ -377,13 +376,12 @@
         w_out.reshape(1, -1),
         labels.reshape(-1, 1),
         cross_v,
-        u_turned,
     )
     (replies,) = call(
         owner_kernel,
         [((ALL_A, EMB), BF16)],
         *operands,
-        scratch=tuple(pltpu.VMEM(x.shape, x.dtype) for x in operands[1:])
+        scratch=tuple(pltpu.VMEM(x.shape, x.dtype) for x in operands[2:])
         + (
             pltpu.VMEM((samples, width), BF16),
             pltpu.VMEM((samples, width), F32),
@@ -391,7 +389,9 @@
             pltpu.VMEM((ALL_A, PEERS), BF16),
             pltpu.VMEM((ALL_A, PEERS), BF16),
             pltpu.VMEM((ALL_A, 2 * PEERS), BF16),
-            pltpu.SemaphoreType.DMA((len(operands) - 1,)),
+            pltpu.VMEM(cross_u.shape[::-1], BF16),
+            pltpu.VMEM(cross_v.shape[::-1], BF16),
+            pltpu.SemaphoreType.DMA((len(operands) - 2,)),
         ),
         flops=2 * 1600 * 10**6,
         hbm=range(1, len(operands)),

time: 140 us -> 139 us (level)
  Pallas kernels: 24 us -> 22.3 us
    pallas_call x7, Pallas kernels: 24 us -> 22.3 us  [call(): pl.pallas_call(kernel, out_shape=[jax.ShapeDtypeStruct(shape, kind) for s...]
  transfers between devices with their start and end apart: 1 -> 1, of which waited for: 1 -> 1; matrix products, arithmetic and copies ran while one was open for 0% -> 0% of each run, Pallas kernels for 6% -> 5%
where the time goes in v1:
time: 139 us
  blocking collectives  77 us (55%)
  Pallas kernels  22.3 us (16%)
  starting transfers between devices  20.6 us (15%)
  waiting for transfers between devices  18.2 us (13%)
    all_to_all x2, blocking collectives, over_rows(): lax.all_to_all(split, 'rows', split_axis=0, concat_axis=0, tiled=True)  61.1 us
    pallas_call x7, Pallas kernels, call(): pl.pallas_call(kernel, out_shape=[jax.ShapeDtypeStruct(shape, kind) for s...  22.3 us
    all_to_all x1, starting transfers between devices, over_rows(): lax.all_to_all(split, 'rows', split_axis=0, concat_axis=0, tiled=True)  20.6 us
    all_to_all x1, waiting for transfers between devices, over_rows(): lax.all_to_all(split, 'rows', split_axis=0, concat_axis=0, tiled=True)  18.2 us
    all_to_all x2, blocking collectives, over_serve(): lax.all_to_all(pieces, 'serve', split_axis=0, concat_axis=0, tiled=True)  15.9 us
  transfers between devices with their start and end apart: 1, of which 1 were waited for; matrix products, arithmetic and copies ran while one was open for 0% of the time, Pallas kernels for 5%

profile of v1, /device:TPU:1, one launch (start us, length us, event | category | flops | bytes accessed | tf_op | source)
XLA Modules:
  0.0 139.1 jit_solution(8776034476156702849)
XLA Ops:
  0.6 0.0 copy-start.7
  0.6 0.0 copy-start.8
  0.7 0.0 copy-start.9
  0.7 4.3 %shard_map.165 = (bf16[1280,128]{1,0:T(8,128)(2,1)}, s32[1,512]{1,0:T(1,128)}) custom-call(s32[1,512]{1,0:T(1,128)} %bitcast.39, s32[1,1536]{1,0:T(1,128)} %bitcast.33, s32[1,512]{1,0:T(1,128)} %bitcast.37, s32[1,512]{1,0:T(1,128)} %bitcast.38, f32[1024,128]{1,0:T(8,128)} %table_ref.1), custom_call_target="tpu_custom_call" | custom-call | flops 1400000000 | bytes 536576 | tf_op jit(solution)/shard_map/pallas_call | solution.py:283
  5.0 20.6 %all-to-all-start = ((bf16[128,5,2,128]{3,2,1,0:T(2,128)(2,1)}), bf16[128,5,2,128]{3,2,1,0:T(2,128)(2,1)S(1)}, u32[]{:S(2)}, u32[]{:S(2)}) async-start(bf16[128,5,2,128]{3,2,1,0:T(2,128)(2,1)} %bitcast.30), calls=%async_computation | async-start | bytes 655360 | tf_op jit(solution)/shard_map/all_to_all | solution.py:295
  25.6 0.0 copy-done.7
  25.7 0.1 copy.18.refs_7_
  25.8 0.0 copy-start.6
  25.8 7.0 %shard_map.166 = (s8[1280,1024]{1,0:T(32,128)(4,1)}, bf16[768,1024]{1,0:T(8,128)(2,1)}, s32[1,1024]{1,0:T(1,128)}, f32[32,1024]{1,0:T(8,128)}) custom-call(s32[1,512]{1,0:T(1,128)} %bitcast.40, s32[1,1536]{1,0:T(1,128)} %bitcast.34, s32[1,512]{1,0:T(1,128)} %get-tuple-element.20.slots_ref, s32[1,1024]{1,0:T(1,128)} %bitcast.35, f32[1024,128]{1,0:T(8,128)} %table_ref.1), custom_call_target="tpu_custom_call" | custom-call | flops 3200000000 | bytes 538624 | tf_op jit(solution)/shard_map/pallas_call | solution.py:283
  32.7 18.2 %all-to-all-done = bf16[128,5,2,128]{3,2,1,0:T(2,128)(2,1)S(1)} async-done(((bf16[128,5,2,128]{3,2,1,0:T(2,128)(2,1)}), bf16[128,5,2,128]{3,2,1,0:T(2,128)(2,1)S(1)}, u32[]{:S(2)}, u32[]{:S(2)}) %all-to-all-start) | async-done | bytes 327712 | tf_op jit(solution)/shard_map/all_to_all | solution.py:295
  51.0 0.0 copy-done.6
  51.0 8.5 %shard_map.167 = bf16[1280,128]{1,0:T(8,128)(2,1)S(1)} custom-call(bf16[1280,128]{1,0:T(8,128)(2,1)S(1)} %bitcast.23, bf16[768,1024]{1,0:T(8,128)(2,1)} %get-tuple-element.21.refs_1_.steps_ref, bf16[128,256]{1,0:T(8,128)(2,1)S(1)} %bitcast.29, bf16[256,128]{1,0:T(8,128)(2,1)S(1)} %copy-done.6, bf16[3456,256]{1,0:T(8,128)(2,1)} %refs_4_.1, ...), custom_call_target="tpu_custom_call" | custom-call | flops 3200000000 | bytes 5598720 | tf_op jit(solution)/shard_map/pallas_call | solution.py:283
  59.5 0.0 copy-start.2
  59.5 0.0 copy-start.3
  59.5 0.0 copy-start.4
  59.5 32.2 %all_to_all.25 = bf16[128,5,2,128]{3,2,1,0:T(2,128)(2,1)S(1)} all-to-all(bf16[128,5,2,128]{3,2,1,0:T(2,128)(2,1)S(1)} %bitcast.24), channel_id=1, replica_groups=mesh['rows'=128,'serve'=4] {'rows'}, dimensions={0} | all-to-all | bytes 655360 | tf_op jit(solution)/shard_map/all_to_all | solution.py:295
  91.7 0.6 shard_map.168
  92.3 9.3 %all_to_all.26.grads_ref = bf16[4,32,1024]{2,1,0:T(8,128)(2,1)S(1)} all-to-all(bf16[4,32,1024]{2,1,0:T(8,128)(2,1)S(1)} %bitcast.25), channel_id=1, replica_groups=mesh['rows'=128,'serve'=4] {'serve'}, dimensions={0} | all-to-all | bytes 524288 | tf_op jit(solution)/shard_map/all_to_all | solution.py:300
  101.7 0.1 shard_map.169
  101.7 6.6 %all_to_all.27.message_ref = f32[4,1,1280]{2,1,0:T(1,128)S(1)} all-to-all(f32[4,1,1280]{2,1,0:T(1,128)S(1)} %get-tuple-element.25), channel_id=1, replica_groups=mesh['rows'=128,'serve'=4] {'serve'}, dimensions={0} | all-to-all | bytes 40960 | tf_op jit(solution)/shard_map/all_to_all | solution.py:300
  108.3 0.0 copy-done
  108.3 0.7 shard_map.170
  109.0 28.9 %all_to_all.28 = bf16[128,3,2,128]{3,2,1,0:T(2,128)(2,1)S(1)} all-to-all(bf16[128,3,2,128]{3,2,1,0:T(2,128)(2,1)S(1)} %bitcast.26), channel_id=1, replica_groups=mesh['rows'=128,'serve'=4] {'rows'}, dimensions={0} | all-to-all | bytes 393216 | tf_op jit(solution)/shard_map/all_to_all | solution.py:295
  137.9 1.2 shard_map.171
  (12 shorter events, 0.0 us)
Async XLA Ops:
  0.6 25.0 %copy-start.7 = (f32[3456]{0:T(1024)S(1)}, f32[3456]{0:T(1024)}, u32[]{:S(2)}) copy-start(f32[3456]{0:T(1024)} %param.25) | copy-start | bytes 41476
  0.6 25.0 %copy-start.8 = (f32[3456]{0:T(1024)S(1)}, f32[3456]{0:T(1024)}, u32[]{:S(2)}) copy-start(f32[3456]{0:T(1024)} %param.26) | copy-start | bytes 41476
  0.7 25.0 %copy-start.9 = (s32[1,128]{1,0:T(1,128)S(1)}, s32[1,128]{1,0:T(1,128)}, u32[]{:S(2)}) copy-start(s32[1,128]{1,0:T(1,128)} %param.21) | copy-start | bytes 1540
  5.0 46.0 %all-to-all-start = ((bf16[128,5,2,128]{3,2,1,0:T(2,128)(2,1)}), bf16[128,5,2,128]{3,2,1,0:T(2,128)(2,1)S(1)}, u32[]{:S(2)}, u32[]{:S(2)}) async-start(bf16[128,5,2,128]{3,2,1,0:T(2,128)(2,1)} %bitcast.30), calls=%async_computation | async-start | bytes 655360 | tf_op jit(solution)/shard_map/all_to_all | solution.py:295
  25.8 25.2 %copy-start.5 = (bf16[1,128,256]{2,1,0:T(8,128)(2,1)S(1)}, bf16[1,128,256]{2,1,0:T(8,128)(2,1)}, u32[]{:S(2)}) copy-start(bf16[1,128,256]{2,1,0:T(8,128)(2,1)} %param.20) | copy-start | bytes 196612
  25.8 25.2 %copy-start.6 = (bf16[256,128]{1,0:T(8,128)(2,1)S(1)}, bf16[256,128]{1,0:T(8,128)(2,1)}, u32[]{:S(2)}) copy-start(bf16[256,128]{1,0:T(8,128)(2,1)} %refs_3_.1) | copy-start | bytes 196612
  51.0 40.7 %copy-start.1 = (s8[1280,1024]{1,0:T(32,128)(4,1)S(1)}, s8[1280,1024]{1,0:T(32,128)(4,1)}, u32[]{:S(2)}) copy-start(s8[1280,1024]{1,0:T(32,128)(4,1)} %get-tuple-element.22.routed_ref) | copy-start | bytes 3932164
  59.5 48.8 %copy-start = (bf16[768,1024]{1,0:T(8,128)(2,1)S(1)}, bf16[768,1024]{1,0:T(8,128)(2,1)}, u32[]{:S(2)}) copy-start(bf16[768,1024]{1,0:T(8,128)(2,1)} %get-tuple-element.21.refs_1_.steps_ref) | copy-start | bytes 4718596
  59.5 48.8 %copy-start.2 = (f32[32,1024]{1,0:T(8,128)S(1)}, f32[32,1024]{1,0:T(8,128)}, u32[]{:S(2)}) copy-start(f32[32,1024]{1,0:T(8,128)} %get-tuple-element.27.table_ref) | copy-start | bytes 393220
  59.5 48.8 %copy-start.3 = (f32[1024]{0:T(1024)S(1)}, f32[1024]{0:T(1024)}, u32[]{:S(2)}) copy-start(f32[1024]{0:T(1024)} %param.15) | copy-start | bytes 12292
  59.5 48.8 %copy-start.4 = (s32[1,1024]{1,0:T(1,128)S(1)}, s32[1,1024]{1,0:T(1,128)}, u32[]{:S(2)}) copy-start(s32[1,1024]{1,0:T(1,128)} %get-tuple-element.28.block_ref) | copy-start | bytes 12292

commit v2 on v1

--- a/solution.py
+++ b/solution.py
@@ -159,17 +159,17 @@
     u_turned_ref, v_turned_ref, sems = refs
     copies = [pltpu.make_async_copy(s, t, sems.at[i]) for i, (s, t) in enumerate(zip(sources, targets))]
     dense_ref, w_bottom_ref, cross_u_ref, bias_ref, w_out_ref, labels_ref, cross_v_ref = targets
-    for copy in copies:
+    for copy in copies[:6]:
         copy.start()
     samples = dense_ref.shape[0]
     peer = iota((PEERS, ALL_A), 0) * ROWS_A
     slot = iota((PEERS, ALL_A), 1)
     name_row = onehot(slot == peer + CAP)
-    chunk = onehot((slot >= peer) & (slot < peer + ROWS_A))
+    chunk = onehot(iota((PEERS, ALL_A), 0) == divide_floor(iota((1, ALL_A), 1), ROWS_A))
     arrived = arrived_ref[...]
     names = dot(name_row, arrived).astype(BF16)
     spread = dot(names, chunk, 0, 0)
-    place = iota((CAP, ALL_A), 1)
+    place = iota((1, ALL_A), 1)
     place = place - divide_floor(place, ROWS_A) * ROWS_A
     picks = iota((CAP, ALL_A), 0) == place
     sample_row = jnp.sum(jnp.where(picks, spread[:CAP], 0.0), axis=0, keepdims=True)
@@ -179,6 +179,7 @@
     member_ref[...] = member_f.T.astype(BF16)
     table_ref[...] = jnp.broadcast_to(table_row, (samples, ALL_A)).T.astype(BF16)
 
+    copies[6].start()
     for copy in copies[:2]:
         copy.wait()
     dense = dense_ref[...]
@@ -187,16 +188,15 @@
     cross_ref[:, :EMB] = (pre_act * sigma).astype(BF16)
     table_t = table_ref[...]
     for t in range(0, TABLES, 2):
-        if t == 14:
-            for copy in copies[2:6]:
-                copy.wait()
-            u_turned_ref[...] = cross_u_ref[...].T
         both = [jnp.where(table_t == t + u, arrived, 0.0).astype(BF16) for u in range(2)]
         cross_ref[:, (t + 1) * EMB : (t + 3) * EMB] = dot(member, jnp.concatenate(both, axis=1)).astype(BF16)
 
+    for copy in copies[2:6]:
+        copy.wait()
+    low_rank = dot(cross_ref[...], cross_u_ref[...]).astype(BF16)
+    u_turned_ref[...] = cross_u_ref[...].T
     copies[6].wait()
     v_turned_ref[...] = cross_v_ref[...].T
-    low_rank = dot(cross_ref[...], cross_u_ref[...]).astype(BF16)
     w_out = w_out_ref[...]
     mixed_ref[...] = (dot(low_rank, cross_v_ref[...]) + (bias_ref[...] + 1.0)) * w_out
     cross_f = cross_ref[...].astype(F32)
@@ -266,11 +266,10 @@
 
 def final_kernel(served_ref, serving_ref, bottom_ref):
     served = served_ref[...]
-    slot = iota((ALL_D, PEERS), 0)
-    peer = iota((ALL_D, PEERS), 1)
-    for r in range(4):
-        pick = onehot(slot == peer * ROWS_D + r)
-        serving_ref[r * EMB : (r + 1) * EMB, :] = dot(served, pick, 0, 0).astype(BF16)
+    slot = iota((ALL_D, PEERS), 0) - iota((ALL_D, PEERS), 1) * ROWS_D
+    picks = jnp.concatenate([onehot(slot == r) for r in range(ROWS_D)], axis=1)
+    lines = dot(served, picks, 0, 0)
+    serving_ref[...] = jnp.concatenate([lines[:, r * PEERS : (r + 1) * PEERS] for r in range(4)], axis=0).astype(BF16)
     line = iota((2 * PEERS, ALL_D), 0)
     slot = iota((2 * PEERS, ALL_D), 1)
     pick = onehot(slot == lax.shift_right_logical(line, 1) * ROWS_D + 4 + (line & 1))

time: 139 us -> 139 us (level)
  no operation moved by 1% of the time
where the time goes in v2:
time: 139 us
  blocking collectives  77 us (55%)
  Pallas kernels  21.9 us (16%)
  starting transfers between devices  20.6 us (15%)
  waiting for transfers between devices  18.2 us (13%)
    all_to_all x2, blocking collectives, over_rows(): lax.all_to_all(split, 'rows', split_axis=0, concat_axis=0, tiled=True)  61.1 us
    pallas_call x7, Pallas kernels, call(): pl.pallas_call(kernel, out_shape=[jax.ShapeDtypeStruct(shape, kind) for s...  21.9 us
    all_to_all x1, starting transfers between devices, over_rows(): lax.all_to_all(split, 'rows', split_axis=0, concat_axis=0, tiled=True)  20.6 us
    all_to_all x1, waiting for transfers between devices, over_rows(): lax.all_to_all(split, 'rows', split_axis=0, concat_axis=0, tiled=True)  18.2 us
    all_to_all x2, blocking collectives, over_serve(): lax.all_to_all(pieces, 'serve', split_axis=0, concat_axis=0, tiled=True)  15.9 us
  transfers between devices with their start and end apart: 1, of which 1 were waited for; matrix products, arithmetic and copies ran while one was open for 0% of the time, Pallas kernels for 5%

profile of v2, /device:TPU:1, one launch (start us, length us, event | category | flops | bytes accessed | tf_op | source)
XLA Modules:
  0.0 138.7 jit_solution(15159684951138177998)
XLA Ops:
  0.6 0.0 copy-start.7
  0.6 0.0 copy-start.8
  0.7 0.0 copy-start.9
  0.7 4.3 %shard_map.165 = (bf16[1280,128]{1,0:T(8,128)(2,1)}, s32[1,512]{1,0:T(1,128)}) custom-call(s32[1,512]{1,0:T(1,128)} %bitcast.39, s32[1,1536]{1,0:T(1,128)} %bitcast.33, s32[1,512]{1,0:T(1,128)} %bitcast.37, s32[1,512]{1,0:T(1,128)} %bitcast.38, f32[1024,128]{1,0:T(8,128)} %table_ref.1), custom_call_target="tpu_custom_call" | custom-call | flops 1400000000 | bytes 536576 | tf_op jit(solution)/shard_map/pallas_call | solution.py:282
  5.0 20.6 %all-to-all-start = ((bf16[128,5,2,128]{3,2,1,0:T(2,128)(2,1)}), bf16[128,5,2,128]{3,2,1,0:T(2,128)(2,1)S(1)}, u32[]{:S(2)}, u32[]{:S(2)}) async-start(bf16[128,5,2,128]{3,2,1,0:T(2,128)(2,1)} %bitcast.30), calls=%async_computation | async-start | bytes 655360 | tf_op jit(solution)/shard_map/all_to_all | solution.py:294
  25.6 0.0 copy-done.7
  25.6 0.0 copy-done.8
  25.7 0.1 copy.18.refs_7_
  25.8 0.0 copy-start.6
  25.8 7.0 %shard_map.166 = (s8[1280,1024]{1,0:T(32,128)(4,1)}, bf16[768,1024]{1,0:T(8,128)(2,1)}, s32[1,1024]{1,0:T(1,128)}, f32[32,1024]{1,0:T(8,128)}) custom-call(s32[1,512]{1,0:T(1,128)} %bitcast.40, s32[1,1536]{1,0:T(1,128)} %bitcast.34, s32[1,512]{1,0:T(1,128)} %get-tuple-element.20.slots_ref, s32[1,1024]{1,0:T(1,128)} %bitcast.35, f32[1024,128]{1,0:T(8,128)} %table_ref.1), custom_call_target="tpu_custom_call" | custom-call | flops 3200000000 | bytes 538624 | tf_op jit(solution)/shard_map/pallas_call | solution.py:282
  32.7 18.2 %all-to-all-done = bf16[128,5,2,128]{3,2,1,0:T(2,128)(2,1)S(1)} async-done(((bf16[128,5,2,128]{3,2,1,0:T(2,128)(2,1)}), bf16[128,5,2,128]{3,2,1,0:T(2,128)(2,1)S(1)}, u32[]{:S(2)}, u32[]{:S(2)}) %all-to-all-start) | async-done | bytes 327712 | tf_op jit(solution)/shard_map/all_to_all | solution.py:294
  51.0 0.0 copy-done.6
  51.0 8.2 %shard_map.167 = bf16[1280,128]{1,0:T(8,128)(2,1)S(1)} custom-call(bf16[1280,128]{1,0:T(8,128)(2,1)S(1)} %bitcast.23, bf16[768,1024]{1,0:T(8,128)(2,1)} %get-tuple-element.21.refs_1_.steps_ref, bf16[128,256]{1,0:T(8,128)(2,1)S(1)} %bitcast.29, bf16[256,128]{1,0:T(8,128)(2,1)S(1)} %copy-done.6, bf16[3456,256]{1,0:T(8,128)(2,1)} %refs_4_.1, ...), custom_call_target="tpu_custom_call" | custom-call | flops 3200000000 | bytes 5598720 | tf_op jit(solution)/shard_map/pallas_call | solution.py:282
  59.2 0.0 copy-start.2
  59.2 0.0 copy-start.3
  59.2 0.0 copy-start.4
  59.3 32.2 %all_to_all.25 = bf16[128,5,2,128]{3,2,1,0:T(2,128)(2,1)S(1)} all-to-all(bf16[128,5,2,128]{3,2,1,0:T(2,128)(2,1)S(1)} %bitcast.24), channel_id=1, replica_groups=mesh['rows'=128,'serve'=4] {'rows'}, dimensions={0} | all-to-all | bytes 655360 | tf_op jit(solution)/shard_map/all_to_all | solution.py:294
  91.5 0.6 shard_map.168
  92.0 9.3 %all_to_all.26.grads_ref = bf16[4,32,1024]{2,1,0:T(8,128)(2,1)S(1)} all-to-all(bf16[4,32,1024]{2,1,0:T(8,128)(2,1)S(1)} %bitcast.25), channel_id=1, replica_groups=mesh['rows'=128,'serve'=4] {'serve'}, dimensions={0} | all-to-all | bytes 524288 | tf_op jit(solution)/shard_map/all_to_all | solution.py:299
  101.4 0.1 shard_map.169
  101.4 6.6 %all_to_all.27.message_ref = f32[4,1,1280]{2,1,0:T(1,128)S(1)} all-to-all(f32[4,1,1280]{2,1,0:T(1,128)S(1)} %get-tuple-element.25), channel_id=1, replica_groups=mesh['rows'=128,'serve'=4] {'serve'}, dimensions={0} | all-to-all | bytes 40960 | tf_op jit(solution)/shard_map/all_to_all | solution.py:299
  108.0 0.7 shard_map.170
  108.7 28.9 %all_to_all.28 = bf16[128,3,2,128]{3,2,1,0:T(2,128)(2,1)S(1)} all-to-all(bf16[128,3,2,128]{3,2,1,0:T(2,128)(2,1)S(1)} %bitcast.26), channel_id=1, replica_groups=mesh['rows'=128,'serve'=4] {'rows'}, dimensions={0} | all-to-all | bytes 393216 | tf_op jit(solution)/shard_map/all_to_all | solution.py:294
  137.6 1.1 shard_map.171
  (12 shorter events, 0.0 us)
Async XLA Ops:
  0.6 25.0 %copy-start.7 = (f32[3456]{0:T(1024)S(1)}, f32[3456]{0:T(1024)}, u32[]{:S(2)}) copy-start(f32[3456]{0:T(1024)} %param.25) | copy-start | bytes 41476
  0.6 25.0 %copy-start.8 = (f32[3456]{0:T(1024)S(1)}, f32[3456]{0:T(1024)}, u32[]{:S(2)}) copy-start(f32[3456]{0:T(1024)} %param.26) | copy-start | bytes 41476
  0.7 25.0 %copy-start.9 = (s32[1,128]{1,0:T(1,128)S(1)}, s32[1,128]{1,0:T(1,128)}, u32[]{:S(2)}) copy-start(s32[1,128]{1,0:T(1,128)} %param.21) | copy-start | bytes 1540
  5.0 46.0 %all-to-all-start = ((bf16[128,5,2,128]{3,2,1,0:T(2,128)(2,1)}), bf16[128,5,2,128]{3,2,1,0:T(2,128)(2,1)S(1)}, u32[]{:S(2)}, u32[]{:S(2)}) async-start(bf16[128,5,2,128]{3,2,1,0:T(2,128)(2,1)} %bitcast.30), calls=%async_computation | async-start | bytes 655360 | tf_op jit(solution)/shard_map/all_to_all | solution.py:294
  25.8 25.2 %copy-start.5 = (bf16[1,128,256]{2,1,0:T(8,128)(2,1)S(1)}, bf16[1,128,256]{2,1,0:T(8,128)(2,1)}, u32[]{:S(2)}) copy-start(bf16[1,128,256]{2,1,0:T(8,128)(2,1)} %param.20) | copy-start | bytes 196612
  25.8 25.2 %copy-start.6 = (bf16[256,128]{1,0:T(8,128)(2,1)S(1)}, bf16[256,128]{1,0:T(8,128)(2,1)}, u32[]{:S(2)}) copy-start(bf16[256,128]{1,0:T(8,128)(2,1)} %refs_3_.1) | copy-start | bytes 196612
  51.0 40.5 %copy-start.1 = (s8[1280,1024]{1,0:T(32,128)(4,1)S(1)}, s8[1280,1024]{1,0:T(32,128)(4,1)}, u32[]{:S(2)}) copy-start(s8[1280,1024]{1,0:T(32,128)(4,1)} %get-tuple-element.22.routed_ref) | copy-start | bytes 3932164
  59.2 48.8 %copy-start = (bf16[768,1024]{1,0:T(8,128)(2,1)S(1)}, bf16[768,1024]{1,0:T(8,128)(2,1)}, u32[]{:S(2)}) copy-start(bf16[768,1024]{1,0:T(8,128)(2,1)} %get-tuple-element.21.refs_1_.steps_ref) | copy-start | bytes 4718596
  59.2 48.8 %copy-start.2 = (f32[32,1024]{1,0:T(8,128)S(1)}, f32[32,1024]{1,0:T(8,128)}, u32[]{:S(2)}) copy-start(f32[32,1024]{1,0:T(8,128)} %get-tuple-element.27.table_ref) | copy-start | bytes 393220
  59.2 48.8 %copy-start.3 = (f32[1024]{0:T(1024)S(1)}, f32[1024]{0:T(1024)}, u32[]{:S(2)}) copy-start(f32[1024]{0:T(1024)} %param.15) | copy-start | bytes 12292
  59.2 48.8 %copy-start.4 = (s32[1,1024]{1,0:T(1,128)S(1)}, s32[1,1024]{1,0:T(1,128)}, u32[]{:S(2)}) copy-start(s32[1,1024]{1,0:T(1,128)} %get-tuple-element.28.block_ref) | copy-start | bytes 12292

commit v3 on v2

--- a/solution.py
+++ b/solution.py
@@ -49,14 +49,14 @@
     return copies
 
 
-def bag_ends(lengths_ref):
-    bags = lengths_ref.shape[1]
-    row_id = iota((bags, bags), 0)
-    col_id = iota((bags, bags), 1)
-    lens = jnp.broadcast_to(lengths_ref[...].astype(F32), (8, bags)).astype(BF16)
-    starts = dot(onehot(col_id < row_id), lens, 1, 1)[:, 0:1].astype(jnp.int32)
-    ends = dot(onehot(col_id <= row_id), lens, 1, 1)[:, 0:1].astype(jnp.int32)
-    return starts, ends
+def bag_ends(lengths_ref, earlier):
+    lens = jnp.broadcast_to(lengths_ref[...].astype(F32), (8, lengths_ref.shape[1]))
+    starts = dot(lens.astype(BF16), earlier)
+    return starts.T[:, 0:1].astype(jnp.int32), (starts + lens).T[:, 0:1].astype(jnp.int32)
+
+
+def earlier_than(count):
+    return onehot(iota((count, count), 0) < iota((count, count), 1))
 
 
 def pool_kernel(
@@ -84,9 +84,11 @@
     touched = table_ref.shape[0]
     for copy in copies[:4]:
         copy.wait()
+    earlier = earlier_than(bags)
+    starts, ends = bag_ends(lengths_ref, earlier)
     owners = owners_ref[...]
     of_owner = jnp.where(iota((PEERS, bags), 0) == owners, 1.0, 0.0)
-    before = dot(of_owner.astype(BF16), onehot(iota((bags, bags), 0) < iota((bags, bags), 1)))
+    before = dot(of_owner.astype(BF16), earlier)
     rank = jnp.sum(before * of_owner, axis=0, keepdims=True).astype(jnp.int32)
     slots = owner_place(owners) * ROWS_A + rank
     slots_ref[...] = slots
@@ -100,7 +102,6 @@
     table = table_ref[...]
     high = table.astype(BF16)
     low = (table - high.astype(F32)).astype(BF16)
-    starts, ends = bag_ends(lengths_ref)
     place = iota((bags, looks), 1)
     in_bag = onehot((place >= starts) & (place < ends))
     lookups = jnp.broadcast_to(lookups_ref[...].astype(F32), (128, looks)).T.astype(jnp.int32)
@@ -112,9 +113,11 @@
         goes = jnp.concatenate([onehot(part == lane + c) for c in range(0, touched, 128)], axis=1)
         sums = sums + dot(in_bag[:, first : first + 512], dot(goes, both).astype(BF16))
     pooled = (sums[:, :EMB] + sums[:, EMB:]).astype(BF16)
-    payload = dot(onehot(iota((ALL_A, bags), 0) == slots), pooled)
-    ninth = onehot(iota((ALL_A, PEERS), 0) == owner_place(iota((ALL_A, PEERS), 1)) * ROWS_A + CAP)
-    out_ref[...] = (payload + dot(ninth, names)).astype(BF16)
+    step = ALL_A // 2
+    for c in range(0, ALL_A, step):
+        ninth = onehot(iota((step, PEERS), 0) + c == iota((1, PEERS), 1) * ROWS_A + CAP)
+        payload = dot(onehot(iota((step, bags), 0) + c == slots), pooled) + dot(ninth, names)
+        out_ref[c : c + step, :] = payload.astype(BF16)
 
 
 def ready_kernel(
@@ -132,7 +135,7 @@
     rows = owners_ref.shape[1]
     bags = slots_ref.shape[1]
     looks = lookups_ref.shape[1]
-    starts, ends = bag_ends(lengths_ref)
+    starts, ends = bag_ends(lengths_ref, earlier_than(bags))
     place = iota((bags, looks), 1)
     in_bag = onehot((place >= starts) & (place < ends))
     of_row = onehot(iota((rows, looks), 0) == lookups_ref[...])

time: 139 us -> 139 us (level)
  no operation moved by 1% of the time
where the time goes in v3:
time: 139 us
  blocking collectives  77 us (55%)
  Pallas kernels  21.8 us (16%)
  starting transfers between devices  20.6 us (15%)
  waiting for transfers between devices  18.1 us (13%)
    all_to_all x2, blocking collectives, over_rows(): lax.all_to_all(split, 'rows', split_axis=0, concat_axis=0, tiled=True)  61.1 us
    pallas_call x7, Pallas kernels, call(): pl.pallas_call(kernel, out_shape=[jax.ShapeDtypeStruct(shape, kind) for s...  21.8 us
    all_to_all x1, starting transfers between devices, over_rows(): lax.all_to_all(split, 'rows', split_axis=0, concat_axis=0, tiled=True)  20.6 us
    all_to_all x1, waiting for transfers between devices, over_rows(): lax.all_to_all(split, 'rows', split_axis=0, concat_axis=0, tiled=True)  18.1 us
    all_to_all x2, blocking collectives, over_serve(): lax.all_to_all(pieces, 'serve', split_axis=0, concat_axis=0, tiled=True)  15.9 us
  transfers between devices with their start and end apart: 1, of which 1 were waited for; matrix products, arithmetic and copies ran while one was open for 0% of the time, Pallas kernels for 5%

profile of v3, /device:TPU:1, one launch (start us, length us, event | category | flops | bytes accessed | tf_op | source)
XLA Modules:
  0.0 138.5 jit_solution(11127212033423568667)
XLA Ops:
  0.6 0.0 copy-start.7
  0.6 0.0 copy-start.8
  0.7 0.0 copy-start.9
  0.7 4.2 %shard_map.165 = (bf16[1280,128]{1,0:T(8,128)(2,1)}, s32[1,512]{1,0:T(1,128)}) custom-call(s32[1,512]{1,0:T(1,128)} %bitcast.39, s32[1,1536]{1,0:T(1,128)} %bitcast.33, s32[1,512]{1,0:T(1,128)} %bitcast.37, s32[1,512]{1,0:T(1,128)} %bitcast.38, f32[1024,128]{1,0:T(8,128)} %table_ref.1), custom_call_target="tpu_custom_call" | custom-call | flops 1400000000 | bytes 536576 | tf_op jit(solution)/shard_map/pallas_call | solution.py:285
  4.8 20.6 %all-to-all-start = ((bf16[128,5,2,128]{3,2,1,0:T(2,128)(2,1)}), bf16[128,5,2,128]{3,2,1,0:T(2,128)(2,1)S(1)}, u32[]{:S(2)}, u32[]{:S(2)}) async-start(bf16[128,5,2,128]{3,2,1,0:T(2,128)(2,1)} %bitcast.30), calls=%async_computation | async-start | bytes 655360 | tf_op jit(solution)/shard_map/all_to_all | solution.py:297
  25.4 0.0 copy-done.7
  25.5 0.1 copy.18.refs_7_
  25.6 0.0 copy-start.6
  25.6 7.1 %shard_map.166 = (s8[1280,1024]{1,0:T(32,128)(4,1)}, bf16[768,1024]{1,0:T(8,128)(2,1)}, s32[1,1024]{1,0:T(1,128)}, f32[32,1024]{1,0:T(8,128)}) custom-call(s32[1,512]{1,0:T(1,128)} %bitcast.40, s32[1,1536]{1,0:T(1,128)} %bitcast.34, s32[1,512]{1,0:T(1,128)} %get-tuple-element.20.slots_ref, s32[1,1024]{1,0:T(1,128)} %bitcast.35, f32[1024,128]{1,0:T(8,128)} %table_ref.1), custom_call_target="tpu_custom_call" | custom-call | flops 3200000000 | bytes 538624 | tf_op jit(solution)/shard_map/pallas_call | solution.py:285
  32.7 18.1 %all-to-all-done = bf16[128,5,2,128]{3,2,1,0:T(2,128)(2,1)S(1)} async-done(((bf16[128,5,2,128]{3,2,1,0:T(2,128)(2,1)}), bf16[128,5,2,128]{3,2,1,0:T(2,128)(2,1)S(1)}, u32[]{:S(2)}, u32[]{:S(2)}) %all-to-all-start) | async-done | bytes 327712 | tf_op jit(solution)/shard_map/all_to_all | solution.py:297
  50.8 8.2 %shard_map.167 = bf16[1280,128]{1,0:T(8,128)(2,1)S(1)} custom-call(bf16[1280,128]{1,0:T(8,128)(2,1)S(1)} %bitcast.23, bf16[768,1024]{1,0:T(8,128)(2,1)} %get-tuple-element.21.refs_1_.steps_ref, bf16[128,256]{1,0:T(8,128)(2,1)S(1)} %bitcast.29, bf16[256,128]{1,0:T(8,128)(2,1)S(1)} %copy-done.6, bf16[3456,256]{1,0:T(8,128)(2,1)} %refs_4_.1, ...), custom_call_target="tpu_custom_call" | custom-call | flops 3200000000 | bytes 5598720 | tf_op jit(solution)/shard_map/pallas_call | solution.py:285
  59.1 0.0 copy-start.2
  59.1 0.0 copy-start.3
  59.1 0.0 copy-start.4
  59.1 32.2 %all_to_all.25 = bf16[128,5,2,128]{3,2,1,0:T(2,128)(2,1)S(1)} all-to-all(bf16[128,5,2,128]{3,2,1,0:T(2,128)(2,1)S(1)} %bitcast.24), channel_id=1, replica_groups=mesh['rows'=128,'serve'=4] {'rows'}, dimensions={0} | all-to-all | bytes 655360 | tf_op jit(solution)/shard_map/all_to_all | solution.py:297
  91.3 0.0 copy-done.1
  91.3 0.6 shard_map.168
  91.9 9.3 %all_to_all.26.grads_ref = bf16[4,32,1024]{2,1,0:T(8,128)(2,1)S(1)} all-to-all(bf16[4,32,1024]{2,1,0:T(8,128)(2,1)S(1)} %bitcast.25), channel_id=1, replica_groups=mesh['rows'=128,'serve'=4] {'serve'}, dimensions={0} | all-to-all | bytes 524288 | tf_op jit(solution)/shard_map/all_to_all | solution.py:302
  101.2 0.1 shard_map.169
  101.3 6.6 %all_to_all.27.message_ref = f32[4,1,1280]{2,1,0:T(1,128)S(1)} all-to-all(f32[4,1,1280]{2,1,0:T(1,128)S(1)} %get-tuple-element.25), channel_id=1, replica_groups=mesh['rows'=128,'serve'=4] {'serve'}, dimensions={0} | all-to-all | bytes 40960 | tf_op jit(solution)/shard_map/all_to_all | solution.py:302
  107.9 0.0 copy-done.2
  107.9 0.7 shard_map.170
  108.6 28.9 %all_to_all.28 = bf16[128,3,2,128]{3,2,1,0:T(2,128)(2,1)S(1)} all-to-all(bf16[128,3,2,128]{3,2,1,0:T(2,128)(2,1)S(1)} %bitcast.26), channel_id=1, replica_groups=mesh['rows'=128,'serve'=4] {'rows'}, dimensions={0} | all-to-all | bytes 393216 | tf_op jit(solution)/shard_map/all_to_all | solution.py:297
  137.5 1.1 shard_map.171
  (12 shorter events, 0.0 us)
Async XLA Ops:
  0.6 24.8 %copy-start.7 = (f32[3456]{0:T(1024)S(1)}, f32[3456]{0:T(1024)}, u32[]{:S(2)}) copy-start(f32[3456]{0:T(1024)} %param.25) | copy-start | bytes 41476
  0.6 24.8 %copy-start.8 = (f32[3456]{0:T(1024)S(1)}, f32[3456]{0:T(1024)}, u32[]{:S(2)}) copy-start(f32[3456]{0:T(1024)} %param.26) | copy-start | bytes 41476
  0.7 24.8 %copy-start.9 = (s32[1,128]{1,0:T(1,128)S(1)}, s32[1,128]{1,0:T(1,128)}, u32[]{:S(2)}) copy-start(s32[1,128]{1,0:T(1,128)} %param.21) | copy-start | bytes 1540
  4.8 46.0 %all-to-all-start = ((bf16[128,5,2,128]{3,2,1,0:T(2,128)(2,1)}), bf16[128,5,2,128]{3,2,1,0:T(2,128)(2,1)S(1)}, u32[]{:S(2)}, u32[]{:S(2)}) async-start(bf16[128,5,2,128]{3,2,1,0:T(2,128)(2,1)} %bitcast.30), calls=%async_computation | async-start | bytes 655360 | tf_op jit(solution)/shard_map/all_to_all | solution.py:297
  25.6 25.2 %copy-start.5 = (bf16[1,128,256]{2,1,0:T(8,128)(2,1)S(1)}, bf16[1,128,256]{2,1,0:T(8,128)(2,1)}, u32[]{:S(2)}) copy-start(bf16[1,128,256]{2,1,0:T(8,128)(2,1)} %param.20) | copy-start | bytes 196612
  25.6 25.2 %copy-start.6 = (bf16[256,128]{1,0:T(8,128)(2,1)S(1)}, bf16[256,128]{1,0:T(8,128)(2,1)}, u32[]{:S(2)}) copy-start(bf16[256,128]{1,0:T(8,128)(2,1)} %refs_3_.1) | copy-start | bytes 196612
  50.8 40.5 %copy-start.1 = (s8[1280,1024]{1,0:T(32,128)(4,1)S(1)}, s8[1280,1024]{1,0:T(32,128)(4,1)}, u32[]{:S(2)}) copy-start(s8[1280,1024]{1,0:T(32,128)(4,1)} %get-tuple-element.22.routed_ref) | copy-start | bytes 3932164
  59.0 48.8 %copy-start = (bf16[768,1024]{1,0:T(8,128)(2,1)S(1)}, bf16[768,1024]{1,0:T(8,128)(2,1)}, u32[]{:S(2)}) copy-start(bf16[768,1024]{1,0:T(8,128)(2,1)} %get-tuple-element.21.refs_1_.steps_ref) | copy-start | bytes 4718596
  59.1 48.8 %copy-start.2 = (f32[32,1024]{1,0:T(8,128)S(1)}, f32[32,1024]{1,0:T(8,128)}, u32[]{:S(2)}) copy-start(f32[32,1024]{1,0:T(8,128)} %get-tuple-element.27.table_ref) | copy-start | bytes 393220
  59.1 48.8 %copy-start.3 = (f32[1024]{0:T(1024)S(1)}, f32[1024]{0:T(1024)}, u32[]{:S(2)}) copy-start(f32[1024]{0:T(1024)} %param.15) | copy-start | bytes 12292
  59.1 48.8 %copy-start.4 = (s32[1,1024]{1,0:T(1,128)S(1)}, s32[1,1024]{1,0:T(1,128)}, u32[]{:S(2)}) copy-start(s32[1,1024]{1,0:T(1,128)} %get-tuple-element.28.block_ref) | copy-start | bytes 12292
